TPU v7x, 32 devices: a whole 2x2x4 slice. The times are simulated.
32 devices in a mesh: groups: 2 (over y), gx: 8 (over z, x), gy: 2 (over core).
Axes of the slice: x: 2, y: 2, z: 4, core: 2. Of those that a mesh axis runs over, the one named last changes fastest.
Arguments:
- offsets: int32 [6, 96, 128, 128], P('groups', 'gx', 'gy'), parts along dimension 0, may hold values from -4 to 3
- fractions: float32 [6, 96, 128, 128], P('groups', 'gx', 'gy'), parts along dimension 0, may hold values from 0 to 1
- masses: float32 [96, 128, 256], P('gx', 'gy', 'groups'), parts along dimension 2, may hold values from 0.3 to 3
- cotangents: float32 [6, 96, 128, 128], P('groups', 'gx', 'gy'), parts along dimension 0, may hold values from -6 to 6
- counts: int32 [192, 16], P(('groups', 'gx'), 'gy'), parts along dimension 0, may hold values from 64 to 1024, as said below
Outputs:
- forces: float32 [6, 160, 144, 128], P('groups', 'gx', 'gy'), parts along dimension 0
- density_adjoint: float32 [320, 144, 128], P(('groups', 'gx'), 'gy'), parts along dimension 0
There are 2 independent parts, one for each index of `groups`. A program takes and returns all parts, laid end to end along the dimension named above; each array names one. Nothing has to cross between parts.
Inputs may be any that keep to these rules, and one draw needn't show every extreme that they name: counts[x, t] live particles in the tile of 8 x 128 lattice sites at plane x and rows 8 * t to 8 * t + 7; the live ones come first in the order y then z; at least one tile is full in every draw.
All inputs are finite; a program needn't handle non-finite values.
Results may differ from a plain program's by a relative error of at most 0.0039.
Values sent between devices are 32-bit elements; how exact they have to be, the bound alone decides.
A program may use at most 64 MiB of HBM per device.

v0:
```python
import jax
import jax.numpy as jnp
from jax import lax
from jax.sharding import PartitionSpec as P

TROWS = 8


def from_behind(block, axis, distance):
    devices = range(lax.axis_size(axis))
    route = [((i - distance) % len(devices), i) for i in devices]
    return lax.ppermute(block, axis, route)


def with_halo(cells, sides, width):
    for axis, dim in sides:
        count = lax.axis_size(axis)
        head = lax.slice_in_dim(cells, 0, width, axis=dim)
        tail = lax.slice_in_dim(cells, cells.shape[dim] - width, cells.shape[dim], axis=dim)
        cells = jnp.concatenate(
            [
                lax.ppermute(tail, axis, [(i, (i + 1) % count) for i in range(count)]),
                cells,
                lax.ppermute(head, axis, [((i + 1) % count, i) for i in range(count)]),
            ],
            axis=dim,
        )
    return cells


def central_x(field):
    return 0.5 * (field[2:, 1:-1] - field[:-2, 1:-1])


def central_y(field):
    return 0.5 * (field[1:-1, 2:] - field[1:-1, :-2])


def central_z(field):
    return (0.5 * (jnp.roll(field, -1, 2) - jnp.roll(field, 1, 2)))[1:-1, 1:-1]


def pad_dim(field, dim, before, after):
    widths = [(0, 0)] * field.ndim
    widths[dim] = (before, after)
    return jnp.pad(field, widths)


def shards(offsets, fractions, masses, cotangents, counts):
    width_x = offsets.shape[1]
    width_y = offsets.shape[2]
    depth = offsets.shape[3]
    blocks = width_y // TROWS
    values = jnp.concatenate([masses[None], cotangents], 0)
    window_x = jnp.arange(9, dtype=jnp.int32)
    window_y = jnp.arange(2 * TROWS, dtype=jnp.int32)
    window_z = jnp.arange(depth, dtype=jnp.int32)
    rows_tile = jnp.arange(TROWS, dtype=jnp.int32)[None, :, None]
    places = (jnp.arange(TROWS, dtype=jnp.int32)[:, None] * depth + window_z[None, :])[None]

    def deposit_plane(plane_idx, mesh):
        shift_part = lax.dynamic_index_in_dim(offsets, plane_idx, 1, keepdims=False).reshape(
            3, blocks, TROWS, depth
        )
        frac_part = lax.dynamic_index_in_dim(fractions, plane_idx, 1, keepdims=False).reshape(
            3, blocks, TROWS, depth
        )
        value_part = lax.dynamic_index_in_dim(values, plane_idx, 1, keepdims=False).reshape(
            4, blocks, TROWS, depth
        )
        tile_counts = lax.dynamic_index_in_dim(counts, plane_idx, 0, keepdims=False)
        live = (places < tile_counts[:, None, None]).astype(jnp.float32)
        value_part = jnp.moveaxis(value_part * live[None], 0, -1)
        cell_x = (shift_part[0] + 4)[..., None]
        weight_x = jnp.where(window_x == cell_x, 1.0 - frac_part[0][..., None], 0.0) + jnp.where(
            window_x == cell_x + 1, frac_part[0][..., None], 0.0
        )
        cell_y = (shift_part[1] + rows_tile + 4)[..., None]
        weight_y = jnp.where(window_y == cell_y, 1.0 - frac_part[1][..., None], 0.0) + jnp.where(
            window_y == cell_y + 1, frac_part[1][..., None], 0.0
        )
        lower_z = ((window_z[None, None, :] + shift_part[2]) % depth)[..., None]
        upper_z = ((window_z[None, None, :] + shift_part[2] + 1) % depth)[..., None]
        weight_z = jnp.where(window_z == lower_z, 1.0 - frac_part[2][..., None], 0.0) + jnp.where(
            window_z == upper_z, frac_part[2][..., None], 0.0
        )
        weight_xy = weight_x[..., :, None] * weight_y[..., None, :]
        left = (weight_xy[..., None, :, :] * value_part[..., :, None, None]).astype(jnp.bfloat16)
        left = left.reshape(blocks, TROWS * depth, 4 * 9 * 2 * TROWS)
        right = weight_z.astype(jnp.bfloat16).reshape(blocks, TROWS * depth, depth)
        product = jnp.einsum("npa,npz->naz", left, right, preferred_element_type=jnp.float32)
        product = product.reshape(blocks, 4, 9, 2 * TROWS, depth)
        lower = jnp.transpose(product[:, :, :, :TROWS], (1, 2, 0, 3, 4)).reshape(
            4, 9, width_y, depth
        )
        upper = jnp.transpose(product[:, :, :, TROWS:], (1, 2, 0, 3, 4)).reshape(
            4, 9, width_y, depth
        )
        piece = pad_dim(lower, 2, 0, 8) + pad_dim(upper, 2, 8, 0)
        current = lax.dynamic_slice_in_dim(mesh, plane_idx, 9, 1)
        return lax.dynamic_update_slice_in_dim(mesh, current + piece, plane_idx, 1)

    mesh = jnp.zeros((4, width_x + 8, width_y + 8, depth), jnp.float32)
    mesh = lax.fori_loop(0, width_x, deposit_plane, mesh)
    from_below = from_behind(mesh[:, width_x + 4 :], "gx", 1)
    from_above = from_behind(mesh[:, :4], "gx", -1)
    inner_x = (
        mesh[:, 4 : width_x + 4]
        + pad_dim(from_below, 1, 0, width_x - 4)
        + pad_dim(from_above, 1, width_x - 4, 0)
    )
    side_below = from_behind(inner_x[:, :, width_y + 4 :], "gy", 1)
    side_above = from_behind(inner_x[:, :, :4], "gy", -1)
    inner = (
        inner_x[:, :, 4 : width_y + 4]
        + pad_dim(side_below, 2, 0, width_y - 4)
        + pad_dim(side_above, 2, width_y - 4, 0)
    )
    extended = with_halo(inner, (("gx", 1), ("gy", 2)), 5)
    density = extended[0]
    forces = -jnp.stack([central_x(density), central_y(density), central_z(density)])
    density_adjoint = central_x(extended[1]) + central_y(extended[2]) + central_z(extended[3])
    return (forces, density_adjoint)


def solution(mesh):
    in_specs = (
        P("groups", "gx", "gy", None),
        P("groups", "gx", "gy", None),
        P("gx", "gy", "groups"),
        P("groups", "gx", "gy", None),
        P(("groups", "gx"), "gy"),
    )
    out_specs = (P("groups", "gx", "gy", None), P(("groups", "gx"), "gy", None))
    return jax.shard_map(shards, mesh=mesh, in_specs=in_specs, out_specs=out_specs, check_vma=False)
```

profile of v0, /device:TPU:0, one launch (start us, length us, event | category | flops | bytes accessed | tf_op | source)
XLA Modules:
  0.0 562.5 jit_solution(10393115624214822224)
XLA Ops:
  4.3 485.4 %while.18 = (s32[]{:T(128)}, f32[4,20,72,128]{3,2,1,0:T(8,128)S(1)}, s32[3,12,64,128]{3,2,1,0:T(8,128)}, f32[3,12,64,128]{3,2,1,0:T(8,128)}, f32[4,12,64,128]{3,...) while((s32[]{:T(128)}, ...), condition=%wide.region_1.2_spmd.clone.clone, body=%wide.region_0.1_spmd.clone.clone.sunk | while | flops 1226867712 | bytes 67060524 | solution.py:104
  9.9 8.5 %multiply_convert_fusion.2 = bf16[8,8,128,4,9,16]{2,1,5,4,3,0:T(8,128)(2,1)} fusion(f32[8,8,128,9,16]{2,1,4,3,0:T(8,128)} %broadcast_multiply_fusion.2, f32[4,12,64,128]{3,2,0,1:T(8,128)} %get-tuple-element.540, s32[]{:T(128)} %get-tuple-element.525, f32[8,8,128]{2,1,0:T(8,128)S(1)} %compare_convert_fusion.2), kind=kLoop, calls=%fused_computation.5.clone.1 | loop fusion | flops 9469952 | bytes 14320128 | tf_op jit(solution)/shard_map/while/body/eval_jaxpr/convert_element_type | solution.py:88
  18.4 14.8 %convert_element_type.79 = bf16[8,1024,576]{1,2,0:T(8,128)(2,1)} reshape(bf16[8,8,128,4,9,16]{2,1,5,4,3,0:T(8,128)(2,1)} %multiply_convert_fusion.2) | data formatting | bytes 18874368 | tf_op jit(solution)/shard_map/while/body/eval_jaxpr/convert_element_type | solution.py:88
  34.1 9.9 %fusion.60 = f32[8,576,128]{2,1,0:T(8,128)S(1)} fusion(bf16[8,1024,576]{1,2,0:T(8,128)(2,1)} %convert_element_type.79, f32[8,1024]{1,0:T(8,128)S(1)} %squeeze.76, s32[8,1024]{1,0:T(8,128)S(1)} %get-tuple-element.508, f32[8,1024]{1,0:T(8,128)S(1)} %broadcast_subtract_fusion.6, s32[8,1024]{1,0:T(8,128)S(1)} %get-tuple-element.509), kind=kOutput, calls=%fused_computation.10.clone.1 | convolution fusion | flops 1214251008 | bytes 11927552 | tf_op jit(solution)/shard_map/while/body/eval_jaxpr/npa,npz->naz/dot_general | solution.py:91
  50.3 8.5 %multiply_convert_fusion.2 = bf16[8,8,128,4,9,16]{2,1,5,4,3,0:T(8,128)(2,1)} fusion(f32[8,8,128,9,16]{2,1,4,3,0:T(8,128)} %broadcast_multiply_fusion.2, f32[4,12,64,128]{3,2,0,1:T(8,128)} %get-tuple-element.540, s32[]{:T(128)} %get-tuple-element.525, f32[8,8,128]{2,1,0:T(8,128)S(1)} %compare_convert_fusion.2), kind=kLoop, calls=%fused_computation.5.clone.1 | loop fusion | flops 9469952 | bytes 14320128 | tf_op jit(solution)/shard_map/while/body/eval_jaxpr/convert_element_type | solution.py:88
  58.8 14.8 %convert_element_type.79 = bf16[8,1024,576]{1,2,0:T(8,128)(2,1)} reshape(bf16[8,8,128,4,9,16]{2,1,5,4,3,0:T(8,128)(2,1)} %multiply_convert_fusion.2) | data formatting | bytes 18874368 | tf_op jit(solution)/shard_map/while/body/eval_jaxpr/convert_element_type | solution.py:88
  74.5 9.9 %fusion.60 = f32[8,576,128]{2,1,0:T(8,128)S(1)} fusion(bf16[8,1024,576]{1,2,0:T(8,128)(2,1)} %convert_element_type.79, f32[8,1024]{1,0:T(8,128)S(1)} %squeeze.76, s32[8,1024]{1,0:T(8,128)S(1)} %get-tuple-element.508, f32[8,1024]{1,0:T(8,128)S(1)} %broadcast_subtract_fusion.6, s32[8,1024]{1,0:T(8,128)S(1)} %get-tuple-element.509), kind=kOutput, calls=%fused_computation.10.clone.1 | convolution fusion | flops 1214251008 | bytes 11927552 | tf_op jit(solution)/shard_map/while/body/eval_jaxpr/npa,npz->naz/dot_general | solution.py:91
  90.8 8.5 %multiply_convert_fusion.2 = bf16[8,8,128,4,9,16]{2,1,5,4,3,0:T(8,128)(2,1)} fusion(f32[8,8,128,9,16]{2,1,4,3,0:T(8,128)} %broadcast_multiply_fusion.2, f32[4,12,64,128]{3,2,0,1:T(8,128)} %get-tuple-element.540, s32[]{:T(128)} %get-tuple-element.525, f32[8,8,128]{2,1,0:T(8,128)S(1)} %compare_convert_fusion.2), kind=kLoop, calls=%fused_computation.5.clone.1 | loop fusion | flops 9469952 | bytes 14320128 | tf_op jit(solution)/shard_map/while/body/eval_jaxpr/convert_element_type | solution.py:88
  99.3 14.8 %convert_element_type.79 = bf16[8,1024,576]{1,2,0:T(8,128)(2,1)} reshape(bf16[8,8,128,4,9,16]{2,1,5,4,3,0:T(8,128)(2,1)} %multiply_convert_fusion.2) | data formatting | bytes 18874368 | tf_op jit(solution)/shard_map/while/body/eval_jaxpr/convert_element_type | solution.py:88
  115.0 9.9 %fusion.60 = f32[8,576,128]{2,1,0:T(8,128)S(1)} fusion(bf16[8,1024,576]{1,2,0:T(8,128)(2,1)} %convert_element_type.79, f32[8,1024]{1,0:T(8,128)S(1)} %squeeze.76, s32[8,1024]{1,0:T(8,128)S(1)} %get-tuple-element.508, f32[8,1024]{1,0:T(8,128)S(1)} %broadcast_subtract_fusion.6, s32[8,1024]{1,0:T(8,128)S(1)} %get-tuple-element.509), kind=kOutput, calls=%fused_computation.10.clone.1 | convolution fusion | flops 1214251008 | bytes 11927552 | tf_op jit(solution)/shard_map/while/body/eval_jaxpr/npa,npz->naz/dot_general | solution.py:91
  131.2 8.5 %multiply_convert_fusion.2 = bf16[8,8,128,4,9,16]{2,1,5,4,3,0:T(8,128)(2,1)} fusion(f32[8,8,128,9,16]{2,1,4,3,0:T(8,128)} %broadcast_multiply_fusion.2, f32[4,12,64,128]{3,2,0,1:T(8,128)} %get-tuple-element.540, s32[]{:T(128)} %get-tuple-element.525, f32[8,8,128]{2,1,0:T(8,128)S(1)} %compare_convert_fusion.2), kind=kLoop, calls=%fused_computation.5.clone.1 | loop fusion | flops 9469952 | bytes 14320128 | tf_op jit(solution)/shard_map/while/body/eval_jaxpr/convert_element_type | solution.py:88
  139.7 14.8 %convert_element_type.79 = bf16[8,1024,576]{1,2,0:T(8,128)(2,1)} reshape(bf16[8,8,128,4,9,16]{2,1,5,4,3,0:T(8,128)(2,1)} %multiply_convert_fusion.2) | data formatting | bytes 18874368 | tf_op jit(solution)/shard_map/while/body/eval_jaxpr/convert_element_type | solution.py:88
  155.4 9.9 %fusion.60 = f32[8,576,128]{2,1,0:T(8,128)S(1)} fusion(bf16[8,1024,576]{1,2,0:T(8,128)(2,1)} %convert_element_type.79, f32[8,1024]{1,0:T(8,128)S(1)} %squeeze.76, s32[8,1024]{1,0:T(8,128)S(1)} %get-tuple-element.508, f32[8,1024]{1,0:T(8,128)S(1)} %broadcast_subtract_fusion.6, s32[8,1024]{1,0:T(8,128)S(1)} %get-tuple-element.509), kind=kOutput, calls=%fused_computation.10.clone.1 | convolution fusion | flops 1214251008 | bytes 11927552 | tf_op jit(solution)/shard_map/while/body/eval_jaxpr/npa,npz->naz/dot_general | solution.py:91
  180.2 14.8 %convert_element_type.79 = bf16[8,1024,576]{1,2,0:T(8,128)(2,1)} reshape(bf16[8,8,128,4,9,16]{2,1,5,4,3,0:T(8,128)(2,1)} %multiply_convert_fusion.2) | data formatting | bytes 18874368 | tf_op jit(solution)/shard_map/while/body/eval_jaxpr/convert_element_type | solution.py:88
  195.9 9.9 %fusion.60 = f32[8,576,128]{2,1,0:T(8,128)S(1)} fusion(bf16[8,1024,576]{1,2,0:T(8,128)(2,1)} %convert_element_type.79, f32[8,1024]{1,0:T(8,128)S(1)} %squeeze.76, s32[8,1024]{1,0:T(8,128)S(1)} %get-tuple-element.508, f32[8,1024]{1,0:T(8,128)S(1)} %broadcast_subtract_fusion.6, s32[8,1024]{1,0:T(8,128)S(1)} %get-tuple-element.509), kind=kOutput, calls=%fused_computation.10.clone.1 | convolution fusion | flops 1214251008 | bytes 11927552 | tf_op jit(solution)/shard_map/while/body/eval_jaxpr/npa,npz->naz/dot_general | solution.py:91
  220.6 14.8 %convert_element_type.79 = bf16[8,1024,576]{1,2,0:T(8,128)(2,1)} reshape(bf16[8,8,128,4,9,16]{2,1,5,4,3,0:T(8,128)(2,1)} %multiply_convert_fusion.2) | data formatting | bytes 18874368 | tf_op jit(solution)/shard_map/while/body/eval_jaxpr/convert_element_type | solution.py:88
  236.3 9.9 %fusion.60 = f32[8,576,128]{2,1,0:T(8,128)S(1)} fusion(bf16[8,1024,576]{1,2,0:T(8,128)(2,1)} %convert_element_type.79, f32[8,1024]{1,0:T(8,128)S(1)} %squeeze.76, s32[8,1024]{1,0:T(8,128)S(1)} %get-tuple-element.508, f32[8,1024]{1,0:T(8,128)S(1)} %broadcast_subtract_fusion.6, s32[8,1024]{1,0:T(8,128)S(1)} %get-tuple-element.509), kind=kOutput, calls=%fused_computation.10.clone.1 | convolution fusion | flops 1214251008 | bytes 11927552 | tf_op jit(solution)/shard_map/while/body/eval_jaxpr/npa,npz->naz/dot_general | solution.py:91
  261.1 14.8 %convert_element_type.79 = bf16[8,1024,576]{1,2,0:T(8,128)(2,1)} reshape(bf16[8,8,128,4,9,16]{2,1,5,4,3,0:T(8,128)(2,1)} %multiply_convert_fusion.2) | data formatting | bytes 18874368 | tf_op jit(solution)/shard_map/while/body/eval_jaxpr/convert_element_type | solution.py:88
  276.8 9.9 %fusion.60 = f32[8,576,128]{2,1,0:T(8,128)S(1)} fusion(bf16[8,1024,576]{1,2,0:T(8,128)(2,1)} %convert_element_type.79, f32[8,1024]{1,0:T(8,128)S(1)} %squeeze.76, s32[8,1024]{1,0:T(8,128)S(1)} %get-tuple-element.508, f32[8,1024]{1,0:T(8,128)S(1)} %broadcast_subtract_fusion.6, s32[8,1024]{1,0:T(8,128)S(1)} %get-tuple-element.509), kind=kOutput, calls=%fused_computation.10.clone.1 | convolution fusion | flops 1214251008 | bytes 11927552 | tf_op jit(solution)/shard_map/while/body/eval_jaxpr/npa,npz->naz/dot_general | solution.py:91
  293.0 8.5 %multiply_convert_fusion.2 = bf16[8,8,128,4,9,16]{2,1,5,4,3,0:T(8,128)(2,1)} fusion(f32[8,8,128,9,16]{2,1,4,3,0:T(8,128)} %broadcast_multiply_fusion.2, f32[4,12,64,128]{3,2,0,1:T(8,128)} %get-tuple-element.540, s32[]{:T(128)} %get-tuple-element.525, f32[8,8,128]{2,1,0:T(8,128)S(1)} %compare_convert_fusion.2), kind=kLoop, calls=%fused_computation.5.clone.1 | loop fusion | flops 9469952 | bytes 14320128 | tf_op jit(solution)/shard_map/while/body/eval_jaxpr/convert_element_type | solution.py:88
  301.5 14.8 %convert_element_type.79 = bf16[8,1024,576]{1,2,0:T(8,128)(2,1)} reshape(bf16[8,8,128,4,9,16]{2,1,5,4,3,0:T(8,128)(2,1)} %multiply_convert_fusion.2) | data formatting | bytes 18874368 | tf_op jit(solution)/shard_map/while/body/eval_jaxpr/convert_element_type | solution.py:88
  317.2 9.9 %fusion.60 = f32[8,576,128]{2,1,0:T(8,128)S(1)} fusion(bf16[8,1024,576]{1,2,0:T(8,128)(2,1)} %convert_element_type.79, f32[8,1024]{1,0:T(8,128)S(1)} %squeeze.76, s32[8,1024]{1,0:T(8,128)S(1)} %get-tuple-element.508, f32[8,1024]{1,0:T(8,128)S(1)} %broadcast_subtract_fusion.6, s32[8,1024]{1,0:T(8,128)S(1)} %get-tuple-element.509), kind=kOutput, calls=%fused_computation.10.clone.1 | convolution fusion | flops 1214251008 | bytes 11927552 | tf_op jit(solution)/shard_map/while/body/eval_jaxpr/npa,npz->naz/dot_general | solution.py:91
  342.0 14.8 %convert_element_type.79 = bf16[8,1024,576]{1,2,0:T(8,128)(2,1)} reshape(bf16[8,8,128,4,9,16]{2,1,5,4,3,0:T(8,128)(2,1)} %multiply_convert_fusion.2) | data formatting | bytes 18874368 | tf_op jit(solution)/shard_map/while/body/eval_jaxpr/convert_element_type | solution.py:88
  357.7 9.9 %fusion.60 = f32[8,576,128]{2,1,0:T(8,128)S(1)} fusion(bf16[8,1024,576]{1,2,0:T(8,128)(2,1)} %convert_element_type.79, f32[8,1024]{1,0:T(8,128)S(1)} %squeeze.76, s32[8,1024]{1,0:T(8,128)S(1)} %get-tuple-element.508, f32[8,1024]{1,0:T(8,128)S(1)} %broadcast_subtract_fusion.6, s32[8,1024]{1,0:T(8,128)S(1)} %get-tuple-element.509), kind=kOutput, calls=%fused_computation.10.clone.1 | convolution fusion | flops 1214251008 | bytes 11927552 | tf_op jit(solution)/shard_map/while/body/eval_jaxpr/npa,npz->naz/dot_general | solution.py:91
  382.4 14.8 %convert_element_type.79 = bf16[8,1024,576]{1,2,0:T(8,128)(2,1)} reshape(bf16[8,8,128,4,9,16]{2,1,5,4,3,0:T(8,128)(2,1)} %multiply_convert_fusion.2) | data formatting | bytes 18874368 | tf_op jit(solution)/shard_map/while/body/eval_jaxpr/convert_element_type | solution.py:88
  398.1 9.9 %fusion.60 = f32[8,576,128]{2,1,0:T(8,128)S(1)} fusion(bf16[8,1024,576]{1,2,0:T(8,128)(2,1)} %convert_element_type.79, f32[8,1024]{1,0:T(8,128)S(1)} %squeeze.76, s32[8,1024]{1,0:T(8,128)S(1)} %get-tuple-element.508, f32[8,1024]{1,0:T(8,128)S(1)} %broadcast_subtract_fusion.6, s32[8,1024]{1,0:T(8,128)S(1)} %get-tuple-element.509), kind=kOutput, calls=%fused_computation.10.clone.1 | convolution fusion | flops 1214251008 | bytes 11927552 | tf_op jit(solution)/shard_map/while/body/eval_jaxpr/npa,npz->naz/dot_general | solution.py:91
  422.9 14.8 %convert_element_type.79 = bf16[8,1024,576]{1,2,0:T(8,128)(2,1)} reshape(bf16[8,8,128,4,9,16]{2,1,5,4,3,0:T(8,128)(2,1)} %multiply_convert_fusion.2) | data formatting | bytes 18874368 | tf_op jit(solution)/shard_map/while/body/eval_jaxpr/convert_element_type | solution.py:88
  438.6 9.9 %fusion.60 = f32[8,576,128]{2,1,0:T(8,128)S(1)} fusion(bf16[8,1024,576]{1,2,0:T(8,128)(2,1)} %convert_element_type.79, f32[8,1024]{1,0:T(8,128)S(1)} %squeeze.76, s32[8,1024]{1,0:T(8,128)S(1)} %get-tuple-element.508, f32[8,1024]{1,0:T(8,128)S(1)} %broadcast_subtract_fusion.6, s32[8,1024]{1,0:T(8,128)S(1)} %get-tuple-element.509), kind=kOutput, calls=%fused_computation.10.clone.1 | convolution fusion | flops 1214251008 | bytes 11927552 | tf_op jit(solution)/shard_map/while/body/eval_jaxpr/npa,npz->naz/dot_general | solution.py:91
  463.3 14.8 %convert_element_type.79 = bf16[8,1024,576]{1,2,0:T(8,128)(2,1)} reshape(bf16[8,8,128,4,9,16]{2,1,5,4,3,0:T(8,128)(2,1)} %multiply_convert_fusion.2) | data formatting | bytes 18874368 | tf_op jit(solution)/shard_map/while/body/eval_jaxpr/convert_element_type | solution.py:88
  479.0 9.9 %fusion.60 = f32[8,576,128]{2,1,0:T(8,128)S(1)} fusion(bf16[8,1024,576]{1,2,0:T(8,128)(2,1)} %convert_element_type.79, f32[8,1024]{1,0:T(8,128)S(1)} %squeeze.76, s32[8,1024]{1,0:T(8,128)S(1)} %get-tuple-element.508, f32[8,1024]{1,0:T(8,128)S(1)} %broadcast_subtract_fusion.6, s32[8,1024]{1,0:T(8,128)S(1)} %get-tuple-element.509), kind=kOutput, calls=%fused_computation.10.clone.1 | convolution fusion | flops 1214251008 | bytes 11927552 | tf_op jit(solution)/shard_map/while/body/eval_jaxpr/npa,npz->naz/dot_general | solution.py:91
  495.9 22.1 %collective-permute-done = f32[4,4,72,128]{3,2,1,0:T(8,128)S(1)} collective-permute-done((f32[4,4,72,128]{3,2,1,0:T(8,128)S(1)}, f32[4,4,72,128]{3,2,1,0:T(8,128)S(1)}, u32[]{:S(2)}, u32[]{:S(2)}) %collective-permute-start) | collective-permute-done | bytes 589856 | tf_op jit(solution)/shard_map/ppermute | solution.py:12
  527.1 24.1 %collective-permute-done.4 = f32[4,5,64,128]{3,2,1,0:T(8,128)S(1)} collective-permute-done((f32[4,5,64,128]{3,2,1,0:T(8,128)S(1)}, f32[4,5,64,128]{3,2,1,0:T(8,128)S(1)}, u32[]{:S(2)}, u32[]{:S(2)}) %collective-permute-start.4) | collective-permute-done | bytes 655392 | tf_op jit(solution)/shard_map/ppermute | solution.py:22
  (255 shorter events, 175.6 us)
Async XLA Ops:
  489.8 28.2 %collective-permute-start = (f32[4,4,72,128]{3,2,1,0:T(8,128)S(1)}, f32[4,4,72,128]{3,2,1,0:T(8,128)S(1)}, u32[]{:S(2)}, u32[]{:S(2)}) collective-permute-start(f32[4,4,72,128]{3,2,1,0:T(8,128)S(1)} %get-tuple-element.419), channel_id=1, source_target_pairs={{14,0},{0,2},{2,4},{4,6},{6,8},{8,10},{10,12},{12,14},{15,1},{1,3}... | collective-permute-start | bytes 1769480 | tf_op jit(solution)/shard_map/ppermute | solution.py:12
  492.8 27.4 %collective-permute-start.1 = (f32[4,4,72,128]{3,2,1,0:T(8,128)S(1)}, f32[4,4,72,128]{3,2,1,0:T(8,128)S(1)}, u32[]{:S(2)}, u32[]{:S(2)}) collective-permute-start(f32[4,4,72,128]{3,2,1,0:T(8,128)S(1)} %get-tuple-element.420), channel_id=1, source_target_pairs={{2,0},{4,2},{6,4},{8,6},{10,8},{12,10},{14,12},{0,14},{3,1},{5,3},... | collective-permute-start | bytes 1769480 | tf_op jit(solution)/shard_map/ppermute | solution.py:12
  520.5 1.4 collective-permute-start.2
  520.5 1.4 collective-permute-start.3
  522.3 28.9 %collective-permute-start.4 = (f32[4,5,64,128]{3,2,1,0:T(8,128)S(1)}, f32[4,5,64,128]{3,2,1,0:T(8,128)S(1)}, u32[]{:S(2)}, u32[]{:S(2)}) collective-permute-start(f32[4,5,64,128]{3,2,1,0:T(8,128)S(1)} %get-tuple-element.425), channel_id=1, source_target_pairs={{0,2},{2,4},{4,6},{6,8},{8,10},{10,12},{12,14},{14,0},{1,3},{3,5},... | collective-permute-start | bytes 1966088 | tf_op jit(solution)/shard_map/ppermute | solution.py:22
  522.7 31.4 %collective-permute-start.5 = (f32[4,5,64,128]{3,2,1,0:T(8,128)S(1)}, f32[4,5,64,128]{3,2,1,0:T(8,128)S(1)}, u32[]{:S(2)}, u32[]{:S(2)}) collective-permute-start(f32[4,5,64,128]{3,2,1,0:T(8,128)S(1)} %get-tuple-element.426), channel_id=1, source_target_pairs={{2,0},{4,2},{6,4},{8,6},{10,8},{12,10},{14,12},{0,14},{3,1},{5,3},... | collective-permute-start | bytes 1966088 | tf_op jit(solution)/shard_map/ppermute | solution.py:24
  554.2 1.7 collective-permute-start.6
  554.3 2.2 collective-permute-start.7
where the time goes:
time: 572 us; the launch traced here: 563 us
  local copies, waits for them, and re-layouts  196 us (34%)
  other arithmetic  180 us (31%)
  matrix products  118 us (21%)
  waiting for transfers between devices  54 us (9%)
  starting transfers between devices  12 us (2%)
    convert_element_type x12, local copies, waits for them, and re-layouts, deposit_plane(): (weight_xy[..., None, :, :] * value_part[..., :, None, None]).astype(jnp....  178 us
    dot_general x12, matrix products, deposit_plane(): jnp.einsum('npa,npz->naz', left, right, preferred_element_type=jnp.float32)  118 us
    convert_element_type x12, other arithmetic, deposit_plane(): (weight_xy[..., None, :, :] * value_part[..., :, None, None]).astype(jnp....  102 us
    mul x12, other arithmetic, deposit_plane(): weight_xy = weight_x[..., :, None] * weight_y[..., None, :]  34.5 us
    ppermute x4, waiting for transfers between devices, from_behind(): return lax.ppermute(block, axis, route)  25.3 us
    ppermute x2, waiting for transfers between devices, with_halo(): lax.ppermute(tail, axis, [(i, (i + 1) % count) for i in range(count)])  25.3 us
  transfers between devices with their start and end apart: 8, of which 8 were waited for; matrix products, arithmetic and copies ran while one was open for 0% of the time, Pallas kernels for 0%

commit v1 on v0

v1 whole, which is shorter than its diff:
```python
import functools

import jax
import jax.numpy as jnp
from jax import lax
from jax.experimental import pallas as pl
from jax.experimental.pallas import tpu as pltpu
from jax.sharding import PartitionSpec as P

TROWS = 8
REACH = 9
WINDOW = 16
PAIR = 2
EDGE = 8


def deposit_kernel(counts_ref, off_ref, frac_ref, mass_ref, cot_ref, out_ref, mesh, prep, left, right):
    x = pl.program_id(0)
    width_y, depth = mass_ref.shape[1:]
    planes, rows_all = mesh.shape[1:3]
    span = PAIR * depth

    @pl.when(x == 0)
    def _():
        mesh[...] = jnp.zeros_like(mesh)

    sub = lax.broadcasted_iota(jnp.int32, (TROWS, depth), 0)
    lane = lax.broadcasted_iota(jnp.int32, (TROWS, depth), 1)
    window_y = lax.broadcasted_iota(jnp.int32, (WINDOW, depth), 0).astype(jnp.float32)
    window_z = lax.broadcasted_iota(jnp.int32, (depth, depth), 0).astype(jnp.float32).astype(jnp.bfloat16)
    zero16 = jnp.zeros((depth, depth), jnp.bfloat16)

    def spread(index, row, count):
        return jnp.broadcast_to(prep[index, row : row + 1, :], (count, depth))

    def build(pair):
        for row in range(PAIR * pair, PAIR * pair + PAIR):
            cols = slice(row * depth, row * depth + depth)
            cell = spread(13, row, WINDOW)
            upper = spread(14, row, WINDOW)
            weight_y = jnp.where(
                window_y == cell, 1.0 - upper, jnp.where(window_y == cell + 1.0, upper, 0.0)
            )
            tops = [weight_y * spread(9 + k, row, WINDOW) for k in range(4)]
            for dx in range(REACH):
                weight_x = spread(dx, row, WINDOW)
                for k in range(4):
                    at = (k * REACH + dx) * WINDOW
                    left[at : at + WINDOW, cols] = (weight_x * tops[k]).astype(jnp.bfloat16)
            low = spread(15, row, depth).astype(jnp.bfloat16)
            high = spread(16, row, depth).astype(jnp.bfloat16)
            one = spread(17, row, depth).astype(jnp.bfloat16)
            two = spread(18, row, depth).astype(jnp.bfloat16)
            right[:, cols] = jnp.where(
                window_z == low, one, jnp.where(window_z == high, two, zero16)
            )

    def tile(t, carry):
        rows = pl.ds(pl.multiple_of(t * TROWS, TROWS), TROWS)
        count = counts_ref[x, t]
        live = sub * depth + lane < count
        shift_x = off_ref[0, 0, rows, :] + 4
        frac_x = frac_ref[0, 0, rows, :]
        for dx in range(REACH):
            prep[dx] = jnp.where(
                shift_x == dx, 1.0 - frac_x, jnp.where(shift_x == dx - 1, frac_x, 0.0)
            )
        prep[9] = jnp.where(live, mass_ref[0, rows, :], 0.0)
        for k in range(3):
            prep[10 + k] = jnp.where(live, cot_ref[k, 0, rows, :], 0.0)
        prep[13] = (off_ref[1, 0, rows, :] + sub + 4).astype(jnp.float32)
        prep[14] = frac_ref[1, 0, rows, :]
        lower = lane + off_ref[2, 0, rows, :]
        prep[15] = ((lower + depth) % depth).astype(jnp.float32)
        prep[16] = ((lower + (depth + 1)) % depth).astype(jnp.float32)
        frac_z = frac_ref[2, 0, rows, :]
        prep[17] = 1.0 - frac_z
        prep[18] = frac_z

        def work(pairs):
            for pair in range(pairs):
                build(pair)
            product = lax.dot_general(
                left[:, : pairs * span],
                right[:, : pairs * span],
                (((1,), (1,)), ((), ())),
                preferred_element_type=jnp.float32,
            ).reshape(4, REACH, WINDOW, depth)
            place = (slice(None), pl.ds(x + 2, REACH), pl.ds(pl.multiple_of(t * TROWS + EDGE, TROWS), WINDOW), slice(None))
            mesh[place] = mesh[place] + product

        most = TROWS // PAIR
        for pairs in range(1, most + 1):
            @pl.when((count > span * (pairs - 1)) & (count <= span * pairs))
            def _():
                work(pairs)

        return carry

    lax.fori_loop(0, width_y // TROWS, tile, 0)

    @pl.when(x == pl.num_programs(0) - 1)
    def _():
        def finish(p, carry):
            out_ref[0, p] = mesh[0, p + 1]
            side = mesh[2, p + 1]
            along = mesh[3, p + 1]
            out_ref[1, p] = 0.5 * (
                (mesh[1, p + 2] - mesh[1, p])
                + (pltpu.roll(side, rows_all - 1, 0) - pltpu.roll(side, 1, 0))
                + (pltpu.roll(along, depth - 1, 1) - pltpu.roll(along, 1, 1))
            )
            return carry

        lax.fori_loop(0, planes - 2, finish, 0)


def deposit(offsets, fractions, masses, cotangents, counts):
    width_x, width_y, depth = masses.shape
    rows_all = width_y + 8 + 2 * EDGE
    planes = width_x + 12
    triple = pl.BlockSpec((3, 1, width_y, depth), lambda i: (0, i, 0, 0))
    return pl.pallas_call(
        deposit_kernel,
        grid=(width_x,),
        out_shape=jax.ShapeDtypeStruct((2, planes - 2, rows_all, depth), jnp.float32),
        in_specs=[
            pl.BlockSpec(memory_space=pltpu.SMEM),
            triple,
            triple,
            pl.BlockSpec((1, width_y, depth), lambda i: (i, 0, 0)),
            triple,
        ],
        out_specs=pl.BlockSpec((2, planes - 2, rows_all, depth), lambda i: (0, 0, 0, 0)),
        scratch_shapes=[
            pltpu.VMEM((4, planes, rows_all, depth), jnp.float32),
            pltpu.VMEM((19, TROWS, depth), jnp.float32),
            pltpu.VMEM((4 * REACH * WINDOW, TROWS * depth), jnp.bfloat16),
            pltpu.VMEM((depth, TROWS * depth), jnp.bfloat16),
        ],
        compiler_params=pltpu.CompilerParams(vmem_limit_bytes=40 << 20),
        name="deposit",
    )(counts, offsets, fractions, masses, cotangents)


def from_behind(block, axis, distance):
    devices = range(lax.axis_size(axis))
    route = [((i - distance) % len(devices), i) for i in devices]
    return lax.ppermute(block, axis, route)


def shards(offsets, fractions, masses, cotangents, counts):
    width_x, width_y, depth = masses.shape
    raw = deposit(offsets, fractions, masses, cotangents, counts)
    below = from_behind(raw[:, :, width_y + 7 : width_y + 17], "gy", 1)
    above = from_behind(raw[:, :, 7:17], "gy", -1)
    rows = raw[:, :, 7 : width_y + 17]
    pad = ((0, 0), (0, 0), (0, width_y), (0, 0)), ((0, 0), (0, 0), (width_y, 0), (0, 0))
    rows = rows + jnp.pad(below, pad[0]) + jnp.pad(above, pad[1])
    behind = from_behind(rows[:, width_x:], "gx", 1)
    ahead = from_behind(rows[:, :10], "gx", -1)
    pad = ((0, 0), (0, width_x), (0, 0), (0, 0)), ((0, 0), (width_x, 0), (0, 0), (0, 0))
    full = rows + jnp.pad(behind, pad[0]) + jnp.pad(ahead, pad[1])
    density = full[0]
    force_x = -0.5 * (density[2:, 1:-1] - density[:-2, 1:-1])
    force_y = -0.5 * (density[1:-1, 2:] - density[1:-1, :-2])
    force_z = -0.5 * (jnp.roll(density, -1, 2) - jnp.roll(density, 1, 2))[1:-1, 1:-1]
    forces = jnp.stack([force_x, force_y[:, :], force_z])
    return forces[:, :, : width_y + 8], full[1, 1:-1, 1 : width_y + 9]


def solution(mesh):
    in_specs = (
        P("groups", "gx", "gy", None),
        P("groups", "gx", "gy", None),
        P("gx", "gy", "groups"),
        P("groups", "gx", "gy", None),
        P(("groups", "gx"), "gy"),
    )
    out_specs = (P("groups", "gx", "gy", None), P(("groups", "gx"), "gy", None))
    return jax.shard_map(shards, mesh=mesh, in_specs=in_specs, out_specs=out_specs, check_vma=False)
```

time: 572 us -> 103 us (0.18); the launches traced: 563 us -> 103 us
  local copies, waits for them, and re-layouts: 196 us -> 8.64 us
  other arithmetic: 180 us -> 2.54 us
  matrix products: 118 us -> 0 us
  Pallas kernels: 0 us -> 52.4 us
  waiting for transfers between devices: 54 us -> 34.5 us
  starting transfers between devices: 12 us -> 3.75 us
    convert_element_type x12 -> x0, local copies, waits for them, and re-layouts: 178 us -> none  [deposit_plane(): (weight_xy[..., None, :, :] * value_part[..., :, None, None]).astype(jnp....]
    dot_general x12 -> x0, matrix products: 118 us -> none  [deposit_plane(): jnp.einsum('npa,npz->naz', left, right, preferred_element_type=jnp.float32)]
    convert_element_type x24 -> x0, other arithmetic: 103 us -> none  [the longest x12 102 us: deposit_plane(): (weight_xy[..., None, :, :] * value_part[..., :, None, None]).astype(jnp....]
    pallas_call x0 -> x1, Pallas kernels: none -> 52.4 us  [deposit(): pl.pallas_call(deposit_kernel, grid=(width_x,), out_shape=jax.ShapeDtypeS...]
    mul x13 -> x0, other arithmetic: 34.5 us -> none  [the longest x12 34.5 us: deposit_plane(): weight_xy = weight_x[..., :, None] * weight_y[..., None, :]]
    ppermute x4 -> x0, waiting for transfers between devices: 28.7 us -> none  [the longest x2 25.3 us: with_halo(): lax.ppermute(tail, axis, [(i, (i + 1) % count) for i in range(count)])]
    add x39 -> x2, other arithmetic: 13.1 us -> 0.36 us  [the longest x1 0.2 us: shards(): full = rows + jnp.pad(behind, pad[0]) + jnp.pad(ahead, pad[1])]
    sub x24 -> x0, other arithmetic: 9.57 us -> none  [the longest x12 9.49 us: deposit_plane(): 1.0 - frac_part[0][..., None]]
  transfers between devices with their start and end apart: 8 -> 4, of which waited for: 8 -> 3; matrix products, arithmetic and copies ran while one was open for 0% -> 1% of each run, Pallas kernels for 0% -> 0%
where the time goes in v1:
time: 103 us
  Pallas kernels  52.4 us (51%)
  waiting for transfers between devices  34.5 us (33%)
  local copies, waits for them, and re-layouts  8.64 us (8%)
  starting transfers between devices  3.75 us (4%)
  other arithmetic  2.54 us (2%)
    pallas_call x1, Pallas kernels, deposit(): pl.pallas_call(deposit_kernel, grid=(width_x,), out_shape=jax.ShapeDtypeS...  52.4 us
    ppermute x4, waiting for transfers between devices, from_behind(): return lax.ppermute(block, axis, route)  34.5 us
    unnamed x9, local copies, waits for them, and re-layouts  5.58 us
    ppermute x4, starting transfers between devices, from_behind(): return lax.ppermute(block, axis, route)  3.75 us
    another operation x2, other arithmetic, shards(): forces = jnp.stack([force_x, force_y[:, :], force_z])  2.18 us
  transfers between devices with their start and end apart: 4, of which 3 were waited for; matrix products, arithmetic and copies ran while one was open for 1% of the time, Pallas kernels for 0%

profile of v1, /device:TPU:0, one launch (start us, length us, event | category | flops | bytes accessed | tf_op | source)
XLA Modules:
  0.0 102.5 jit_solution(5923691119989539384)
XLA Ops:
  0.6 0.8 copy.8.counts_ref
  1.4 0.0 copy-start
  1.4 1.3 %copy-done = s32[3,12,64,128]{3,2,1,0:T(8,128)S(1)} copy-done((s32[3,12,64,128]{3,2,1,0:T(8,128)S(1)}, s32[3,12,64,128]{3,2,1,0:T(8,128)}, u32[]{:S(2)}) %copy-start) | copy-done | bytes 1179672
  2.7 0.0 copy-start.1
  2.7 1.3 %copy-done.1 = f32[3,12,64,128]{3,2,1,0:T(8,128)S(1)} copy-done((f32[3,12,64,128]{3,2,1,0:T(8,128)S(1)}, f32[3,12,64,128]{3,2,1,0:T(8,128)}, u32[]{:S(2)}) %copy-start.1) | copy-done | bytes 1179672
  3.9 0.0 copy-start.2
  3.9 1.3 %copy-done.2 = f32[3,12,64,128]{3,2,1,0:T(8,128)S(1)} copy-done((f32[3,12,64,128]{3,2,1,0:T(8,128)S(1)}, f32[3,12,64,128]{3,2,1,0:T(8,128)}, u32[]{:S(2)}) %copy-start.2) | copy-done | bytes 1179672
  5.2 0.0 copy-start.3
  5.2 1.0 copy-done.3
  6.2 52.4 %deposit.1 = f32[2,22,88,128]{3,2,1,0:T(8,128)S(1)} custom-call(s32[12,8]{1,0:T(8,128)S(1)} %copy.8.counts_ref, s32[3,12,64,128]{3,2,1,0:T(8,128)S(1)} %copy-done, f32[3,12,64,128]{3,2,1,0:T(8,128)S(1)} %copy-done.1, f32[12,64,128]{2,1,0:T(8,128)S(1)} %copy-done.3, f32[3,12,64,128]{3,2,1,0:T(8,128)S(1)} %copy-done.2), custom_call_target="tpu_custom_call" | custom-call | tf_op jit(solution)/shard_map/deposit/pallas_call | solution.py:123
  58.6 0.1 fusion.8
  58.7 1.5 %collective-permute-start = (f32[2,22,10,128]{3,2,1,0:T(8,128)S(1)}, f32[2,22,10,128]{3,2,1,0:T(8,128)S(1)}, u32[]{:S(2)}, u32[]{:S(2)}) collective-permute-start(f32[2,22,10,128]{3,2,1,0:T(8,128)S(1)} %get-tuple-element.2), channel_id=1, source_target_pairs={{1,0},{0,1},{3,2},{2,3},{5,4},{4,5},{7,6},{6,7},{9,8},{8,9},{11,10... | collective-permute-start | bytes 675848 | tf_op jit(solution)/shard_map/ppermute | solution.py:149
  60.2 0.1 collective-permute-start.1
  60.3 1.2 %collective-permute-done = f32[2,22,10,128]{3,2,1,0:T(8,128)S(1)} collective-permute-done((f32[2,22,10,128]{3,2,1,0:T(8,128)S(1)}, f32[2,22,10,128]{3,2,1,0:T(8,128)S(1)}, u32[]{:S(2)}, u32[]{:S(2)}) %collective-permute-start) | collective-permute-done | bytes 225312 | tf_op jit(solution)/shard_map/ppermute | solution.py:149
  61.5 0.5 collective-permute-done.1
  62.0 0.2 fusion
  62.2 0.1 fusion.9
  62.3 0.6 copy.11
  62.9 0.1 collective-permute-start.3
  63.0 0.6 copy.9
  63.6 2.1 %collective-permute-start.2 = (f32[2,10,74,128]{3,0,2,1:T(2,128)S(1)}, f32[2,10,74,128]{3,0,2,1:T(2,128)S(1)}, u32[]{:S(2)}, u32[]{:S(2)}) collective-permute-start(f32[2,10,74,128]{3,0,2,1:T(2,128)S(1)} %copy.9), channel_id=1, source_target_pairs={{14,0},{0,2},{2,4},{4,6},{6,8},{8,10},{10,12},{12,14},{15,1},{1,3}... | collective-permute-start | bytes 2273288 | tf_op jit(solution)/shard_map/ppermute | solution.py:149
  65.7 32.8 %collective-permute-done.3 = f32[2,10,74,128]{3,0,2,1:T(2,128)S(1)} collective-permute-done((f32[2,10,74,128]{3,0,2,1:T(2,128)S(1)}, f32[2,10,74,128]{3,0,2,1:T(2,128)S(1)}, u32[]{:S(2)}, u32[]{:S(2)}) %collective-permute-start.3) | collective-permute-done | bytes 757792 | tf_op jit(solution)/shard_map/ppermute | solution.py:149
  98.4 0.1 copy.12
  98.5 0.0 collective-permute-done.2
  98.5 0.1 copy.10
  98.6 0.2 pad_add_fusion
  98.8 0.9 slice_bitcast_fusion.1
  99.7 0.1 slice_bitcast_fusion
  99.7 0.3 fusion.11
  100.0 0.3 fusion.10
  100.3 0.7 fusion.7
  101.0 1.5 %pad_maximum_fusion = f32[3,20,72,128]{3,2,1,0:T(8,128)} fusion(f32[1,20,72,128]{3,2,1,0:T(8,128)S(1)} %get-tuple-element.12, f32[1,20,72,128]{3,2,1,0:T(8,128)S(1)} %get-tuple-element.7, f32[1,20,72,128]{3,2,1,0:T(8,128)S(1)} %get-tuple-element.6), kind=kLoop, calls=%fused_computation | loop fusion | flops 1105920 | bytes 4423680 | tf_op jit(solution)/shard_map/stack | solution.py:168
Async XLA Ops:
  1.4 1.3 %copy-start = (s32[3,12,64,128]{3,2,1,0:T(8,128)S(1)}, s32[3,12,64,128]{3,2,1,0:T(8,128)}, u32[]{:S(2)}) copy-start(s32[3,12,64,128]{3,2,1,0:T(8,128)} %off_ref.1) | copy-start | bytes 3538948
  2.7 1.3 %copy-start.1 = (f32[3,12,64,128]{3,2,1,0:T(8,128)S(1)}, f32[3,12,64,128]{3,2,1,0:T(8,128)}, u32[]{:S(2)}) copy-start(f32[3,12,64,128]{3,2,1,0:T(8,128)} %frac_ref.1) | copy-start | bytes 3538948
  3.9 1.3 %copy-start.2 = (f32[3,12,64,128]{3,2,1,0:T(8,128)S(1)}, f32[3,12,64,128]{3,2,1,0:T(8,128)}, u32[]{:S(2)}) copy-start(f32[3,12,64,128]{3,2,1,0:T(8,128)} %cot_ref.1) | copy-start | bytes 3538948
  5.2 1.0 copy-start.3
  58.7 2.8 %collective-permute-start = (f32[2,22,10,128]{3,2,1,0:T(8,128)S(1)}, f32[2,22,10,128]{3,2,1,0:T(8,128)S(1)}, u32[]{:S(2)}, u32[]{:S(2)}) collective-permute-start(f32[2,22,10,128]{3,2,1,0:T(8,128)S(1)} %get-tuple-element.2), channel_id=1, source_target_pairs={{1,0},{0,1},{3,2},{2,3},{5,4},{4,5},{7,6},{6,7},{9,8},{8,9},{11,10... | collective-permute-start | bytes 675848 | tf_op jit(solution)/shard_map/ppermute | solution.py:149
  60.2 1.8 %collective-permute-start.1 = (f32[2,22,10,128]{3,2,1,0:T(8,128)S(1)}, f32[2,22,10,128]{3,2,1,0:T(8,128)S(1)}, u32[]{:S(2)}, u32[]{:S(2)}) collective-permute-start(f32[2,22,10,128]{3,2,1,0:T(8,128)S(1)} %get-tuple-element.3), channel_id=1, source_target_pairs={{1,0},{0,1},{3,2},{2,3},{5,4},{4,5},{7,6},{6,7},{9,8},{8,9},{11,10... | collective-permute-start | bytes 675848 | tf_op jit(solution)/shard_map/ppermute | solution.py:149
  62.9 35.5 %collective-permute-start.3 = (f32[2,10,74,128]{3,0,2,1:T(2,128)S(1)}, f32[2,10,74,128]{3,0,2,1:T(2,128)S(1)}, u32[]{:S(2)}, u32[]{:S(2)}) collective-permute-start(f32[2,10,74,128]{3,0,2,1:T(2,128)S(1)} %copy.11), channel_id=1, source_target_pairs={{2,0},{4,2},{6,4},{8,6},{10,8},{12,10},{14,12},{0,14},{3,1},{5,3},... | collective-permute-start | bytes 2273288 | tf_op jit(solution)/shard_map/ppermute | solution.py:149
  63.6 34.9 %collective-permute-start.2 = (f32[2,10,74,128]{3,0,2,1:T(2,128)S(1)}, f32[2,10,74,128]{3,0,2,1:T(2,128)S(1)}, u32[]{:S(2)}, u32[]{:S(2)}) collective-permute-start(f32[2,10,74,128]{3,0,2,1:T(2,128)S(1)} %copy.9), channel_id=1, source_target_pairs={{14,0},{0,2},{2,4},{4,6},{6,8},{8,10},{10,12},{12,14},{15,1},{1,3}... | collective-permute-start | bytes 2273288 | tf_op jit(solution)/shard_map/ppermute | solution.py:149

commit v2 on v1

--- a/solution.py
+++ b/solution.py
@@ -138,7 +138,7 @@
             pltpu.VMEM((4 * REACH * WINDOW, TROWS * depth), jnp.bfloat16),
             pltpu.VMEM((depth, TROWS * depth), jnp.bfloat16),
         ],
-        compiler_params=pltpu.CompilerParams(vmem_limit_bytes=40 << 20),
+        compiler_params=pltpu.CompilerParams(vmem_limit_bytes=56 << 20),
         name="deposit",
     )(counts, offsets, fractions, masses, cotangents)
 
@@ -149,6 +149,20 @@
     return lax.ppermute(block, axis, route)
 
 
+def send_x(field, width_x, low, high):
+    behind = from_behind(field[width_x + low : width_x + low + 9], "gx", 1)
+    ahead = from_behind(field[high : high + 9], "gx", -1)
+    return behind, ahead
+
+
+def join_x(field, behind, ahead, width_x, low, high):
+    return (
+        field
+        + jnp.pad(behind, ((low, width_x + 1 - low), (0, 0), (0, 0)))
+        + jnp.pad(ahead, ((width_x + high, 1 - high), (0, 0), (0, 0)))
+    )
+
+
 def shards(offsets, fractions, masses, cotangents, counts):
     width_x, width_y, depth = masses.shape
     raw = deposit(offsets, fractions, masses, cotangents, counts)
@@ -157,16 +171,14 @@
     rows = raw[:, :, 7 : width_y + 17]
     pad = ((0, 0), (0, 0), (0, width_y), (0, 0)), ((0, 0), (0, 0), (width_y, 0), (0, 0))
     rows = rows + jnp.pad(below, pad[0]) + jnp.pad(above, pad[1])
-    behind = from_behind(rows[:, width_x:], "gx", 1)
-    ahead = from_behind(rows[:, :10], "gx", -1)
-    pad = ((0, 0), (0, width_x), (0, 0), (0, 0)), ((0, 0), (width_x, 0), (0, 0), (0, 0))
-    full = rows + jnp.pad(behind, pad[0]) + jnp.pad(ahead, pad[1])
-    density = full[0]
+    density = rows[0]
+    adjoint = rows[1, :, 1 : width_y + 9]
+    density = join_x(density, *send_x(density, width_x, 0, 1), width_x, 0, 1)
+    adjoint = join_x(adjoint, *send_x(adjoint, width_x, 1, 0), width_x, 1, 0)
     force_x = -0.5 * (density[2:, 1:-1] - density[:-2, 1:-1])
     force_y = -0.5 * (density[1:-1, 2:] - density[1:-1, :-2])
     force_z = -0.5 * (jnp.roll(density, -1, 2) - jnp.roll(density, 1, 2))[1:-1, 1:-1]
-    forces = jnp.stack([force_x, force_y[:, :], force_z])
-    return forces[:, :, : width_y + 8], full[1, 1:-1, 1 : width_y + 9]
+    return jnp.stack([force_x, force_y, force_z]), adjoint[1:-1]
 
 
 def solution(mesh):

time: 103 us -> 99.2 us (0.963); the launches traced: 103 us -> 100 us
  starting transfers between devices: 3.75 us -> 19 us
  waiting for transfers between devices: 34.5 us -> 25.5 us
  Pallas kernels: 52.4 us -> 46.6 us
  local copies, waits for them, and re-layouts: 8.64 us -> 3.41 us
  other arithmetic: 2.54 us -> 4.99 us
    ppermute x4 -> x6, starting transfers between devices: 3.75 us -> 19 us  [from_behind(): return lax.ppermute(block, axis, route)]
    ppermute x4 -> x6, waiting for transfers between devices: 34.5 us -> 25.5 us  [from_behind(): return lax.ppermute(block, axis, route)]
    pallas_call x1, Pallas kernels: 52.4 us -> 46.6 us  [deposit(): pl.pallas_call(deposit_kernel, grid=(width_x,), out_shape=jax.ShapeDtypeS...]
    unnamed x9 -> x1, local copies, waits for them, and re-layouts: 5.58 us -> 1.36 us
    add x1, other arithmetic: 0.16 us -> 1.74 us  [shards(): rows = rows + jnp.pad(below, pad[0]) + jnp.pad(above, pad[1])]
    slice x1, local copies, waits for them, and re-layouts: 0.08 us -> 1.29 us  [shards(): below = from_behind(raw[:, :, width_y + 7:width_y + 17], 'gy', 1)]
    slice x3 -> x2, local copies, waits for them, and re-layouts: 1.29 us -> 0.1 us  [send_x(): behind = from_behind(field[width_x + low:width_x + low + 9], 'gx', 1)]
  transfers between devices with their start and end apart: 4 -> 6, of which waited for: 3 -> 6; matrix products, arithmetic and copies ran while one was open for 1% -> 1% of each run, Pallas kernels for 0% -> 0%
where the time goes in v2:
time: 99.2 us; the launch traced here: 100 us
  Pallas kernels  46.6 us (47%)
  waiting for transfers between devices  25.5 us (26%)
  starting transfers between devices  19 us (19%)
  other arithmetic  4.99 us (5%)
  local copies, waits for them, and re-layouts  3.41 us (3%)
    pallas_call x1, Pallas kernels, deposit(): pl.pallas_call(deposit_kernel, grid=(width_x,), out_shape=jax.ShapeDtypeS...  46.6 us
    ppermute x6, waiting for transfers between devices, from_behind(): return lax.ppermute(block, axis, route)  25.5 us
    ppermute x6, starting transfers between devices, from_behind(): return lax.ppermute(block, axis, route)  19 us
    another operation x2, other arithmetic, shards(): return (jnp.stack([force_x, force_y, force_z]), adjoint[1:-1])  2.18 us
  transfers between devices with their start and end apart: 6, of which 6 were waited for; matrix products, arithmetic and copies ran while one was open for 1% of the time, Pallas kernels for 0%

profile of v2, /device:TPU:0, one launch (start us, length us, event | category | flops | bytes accessed | tf_op | source)
XLA Modules:
  0.0 100.2 jit_solution(7128862312292041950)
XLA Ops:
  0.6 1.4 %copy.7.counts_ref = s32[12,8]{1,0:T(8,128)} copy(s32[12,8]{0,1:T(8,128)} %param.9) | data formatting | bytes 768 | tf_op args[4]
  2.0 46.6 %deposit.1 = f32[2,22,88,128]{3,2,1,0:T(8,128)} custom-call(s32[12,8]{1,0:T(8,128)} %copy.7.counts_ref, s32[3,12,64,128]{3,2,1,0:T(8,128)} %off_ref.1, f32[3,12,64,128]{3,2,1,0:T(8,128)} %frac_ref.1, f32[12,64,128]{2,1,0:T(8,128)} %mass_ref.1, f32[3,12,64,128]{3,2,1,0:T(8,128)} %cot_ref.1), custom_call_target="tpu_custom_call" | custom-call | tf_op jit(solution)/shard_map/deposit/pallas_call | solution.py:123
  48.6 1.3 %fusion.10 = (f32[2,22,10,128]{3,2,1,0:T(8,128)S(1)}, f32[2,22,10,128]{3,2,1,0:T(8,128)S(1)}) fusion(f32[2,22,88,128]{3,2,1,0:T(8,128)} %deposit.1), kind=kLoop, calls=%fused_computation.24 | loop fusion | bytes 901120 | tf_op jit(solution)/shard_map/slice | solution.py:169
  49.9 0.8 collective-permute-start
  50.7 0.1 collective-permute-start.1
  50.7 1.2 %collective-permute-done = f32[2,22,10,128]{3,2,1,0:T(8,128)S(1)} collective-permute-done((f32[2,22,10,128]{3,2,1,0:T(8,128)S(1)}, f32[2,22,10,128]{3,2,1,0:T(8,128)S(1)}, u32[]{:S(2)}, u32[]{:S(2)}) %collective-permute-start) | collective-permute-done | bytes 225312 | tf_op jit(solution)/shard_map/ppermute | solution.py:149
  52.0 0.5 collective-permute-done.1
  52.5 1.7 %fusion = f32[2,22,74,128]{3,2,1,0:T(8,128)S(1)} fusion(f32[2,22,88,128]{3,2,1,0:T(8,128)} %deposit.1, f32[2,22,10,128]{3,2,1,0:T(8,128)S(1)} %collective-permute-done.1, f32[2,22,10,128]{3,2,1,0:T(8,128)S(1)} %collective-permute-done), kind=kLoop, calls=%fused_computation.2 | loop fusion | flops 833536 | bytes 3784704 | tf_op jit(solution)/shard_map/add | solution.py:173
  54.3 10.6 %collective-permute-start.4 = (f32[9,72,128]{2,1,0:T(8,128)S(1)}, f32[9,72,128]{2,1,0:T(8,128)S(1)}, u32[]{:S(2)}, u32[]{:S(2)}) collective-permute-start(f32[9,72,128]{2,1,0:T(8,128)S(1)} %get-tuple-element.4), channel_id=1, source_target_pairs={{14,0},{0,2},{2,4},{4,6},{6,8},{8,10},{10,12},{12,14},{15,1},{1,3}... | collective-permute-start | bytes 995336 | tf_op jit(solution)/shard_map/ppermute | solution.py:149
  64.9 2.8 %collective-permute-start.5 = (f32[9,72,128]{2,1,0:T(8,128)S(1)}, f32[9,72,128]{2,1,0:T(8,128)S(1)}, u32[]{:S(2)}, u32[]{:S(2)}) collective-permute-start(f32[9,72,128]{2,1,0:T(8,128)S(1)} %get-tuple-element.5), channel_id=1, source_target_pairs={{2,0},{4,2},{6,4},{8,6},{10,8},{12,10},{14,12},{0,14},{3,1},{5,3},... | collective-permute-start | bytes 995336 | tf_op jit(solution)/shard_map/ppermute | solution.py:149
  67.7 0.1 collective-permute-start.2
  67.8 4.7 %collective-permute-start.3 = (f32[9,74,128]{2,1,0:T(8,128)S(1)}, f32[9,74,128]{2,1,0:T(8,128)S(1)}, u32[]{:S(2)}, u32[]{:S(2)}) collective-permute-start(f32[9,74,128]{2,1,0:T(8,128)S(1)} %get-tuple-element.7), channel_id=1, source_target_pairs={{2,0},{4,2},{6,4},{8,6},{10,8},{12,10},{14,12},{0,14},{3,1},{5,3},... | collective-permute-start | bytes 1022984 | tf_op jit(solution)/shard_map/ppermute | solution.py:149
  72.5 0.1 slice_bitcast_fusion.1
  72.6 15.5 %collective-permute-done.4 = f32[9,72,128]{2,1,0:T(8,128)S(1)} collective-permute-done((f32[9,72,128]{2,1,0:T(8,128)S(1)}, f32[9,72,128]{2,1,0:T(8,128)S(1)}, u32[]{:S(2)}, u32[]{:S(2)}) %collective-permute-start.4) | collective-permute-done | bytes 331808 | tf_op jit(solution)/shard_map/ppermute | solution.py:149
  88.0 2.5 %collective-permute-done.5 = f32[9,72,128]{2,1,0:T(8,128)S(1)} collective-permute-done((f32[9,72,128]{2,1,0:T(8,128)S(1)}, f32[9,72,128]{2,1,0:T(8,128)S(1)}, u32[]{:S(2)}, u32[]{:S(2)}) %collective-permute-start.5) | collective-permute-done | bytes 331808 | tf_op jit(solution)/shard_map/ppermute | solution.py:149
  90.6 1.0 pad_add_fusion
  91.5 3.6 %collective-permute-done.2 = f32[9,74,128]{2,1,0:T(8,128)S(1)} collective-permute-done((f32[9,74,128]{2,1,0:T(8,128)S(1)}, f32[9,74,128]{2,1,0:T(8,128)S(1)}, u32[]{:S(2)}, u32[]{:S(2)}) %collective-permute-start.2) | collective-permute-done | bytes 341024 | tf_op jit(solution)/shard_map/ppermute | solution.py:149
  95.1 2.2 %collective-permute-done.3 = f32[9,74,128]{2,1,0:T(8,128)S(1)} collective-permute-done((f32[9,74,128]{2,1,0:T(8,128)S(1)}, f32[9,74,128]{2,1,0:T(8,128)S(1)}, u32[]{:S(2)}, u32[]{:S(2)}) %collective-permute-start.3) | collective-permute-done | bytes 341024 | tf_op jit(solution)/shard_map/ppermute | solution.py:149
  97.3 0.1 fusion.2
  97.4 0.3 fusion.12
  97.7 0.3 fusion.11
  98.0 0.7 fusion.9
  98.7 1.5 %pad_maximum_fusion = f32[3,20,72,128]{3,2,1,0:T(8,128)} fusion(f32[1,20,72,128]{3,2,1,0:T(8,128)S(1)} %get-tuple-element.14, f32[1,20,72,128]{3,2,1,0:T(8,128)S(1)} %get-tuple-element.9, f32[1,20,72,128]{3,2,1,0:T(8,128)S(1)} %get-tuple-element.8), kind=kLoop, calls=%fused_computation | loop fusion | flops 1105920 | bytes 4423680 | tf_op jit(solution)/shard_map/stack | solution.py:181
  (2 shorter events, 0.1 us)
Async XLA Ops:
  49.9 2.1 %collective-permute-start = (f32[2,22,10,128]{3,2,1,0:T(8,128)S(1)}, f32[2,22,10,128]{3,2,1,0:T(8,128)S(1)}, u32[]{:S(2)}, u32[]{:S(2)}) collective-permute-start(f32[2,22,10,128]{3,2,1,0:T(8,128)S(1)} %get-tuple-element.2), channel_id=1, source_target_pairs={{1,0},{0,1},{3,2},{2,3},{5,4},{4,5},{7,6},{6,7},{9,8},{8,9},{11,10... | collective-permute-start | bytes 675848 | tf_op jit(solution)/shard_map/ppermute | solution.py:149
  50.7 1.8 %collective-permute-start.1 = (f32[2,22,10,128]{3,2,1,0:T(8,128)S(1)}, f32[2,22,10,128]{3,2,1,0:T(8,128)S(1)}, u32[]{:S(2)}, u32[]{:S(2)}) collective-permute-start(f32[2,22,10,128]{3,2,1,0:T(8,128)S(1)} %get-tuple-element.3), channel_id=1, source_target_pairs={{1,0},{0,1},{3,2},{2,3},{5,4},{4,5},{7,6},{6,7},{9,8},{8,9},{11,10... | collective-permute-start | bytes 675848 | tf_op jit(solution)/shard_map/ppermute | solution.py:149
  54.3 33.8 %collective-permute-start.4 = (f32[9,72,128]{2,1,0:T(8,128)S(1)}, f32[9,72,128]{2,1,0:T(8,128)S(1)}, u32[]{:S(2)}, u32[]{:S(2)}) collective-permute-start(f32[9,72,128]{2,1,0:T(8,128)S(1)} %get-tuple-element.4), channel_id=1, source_target_pairs={{14,0},{0,2},{2,4},{4,6},{6,8},{8,10},{10,12},{12,14},{15,1},{1,3}... | collective-permute-start | bytes 995336 | tf_op jit(solution)/shard_map/ppermute | solution.py:149
  64.9 25.7 %collective-permute-start.5 = (f32[9,72,128]{2,1,0:T(8,128)S(1)}, f32[9,72,128]{2,1,0:T(8,128)S(1)}, u32[]{:S(2)}, u32[]{:S(2)}) collective-permute-start(f32[9,72,128]{2,1,0:T(8,128)S(1)} %get-tuple-element.5), channel_id=1, source_target_pairs={{2,0},{4,2},{6,4},{8,6},{10,8},{12,10},{14,12},{0,14},{3,1},{5,3},... | collective-permute-start | bytes 995336 | tf_op jit(solution)/shard_map/ppermute | solution.py:149
  67.7 27.4 %collective-permute-start.2 = (f32[9,74,128]{2,1,0:T(8,128)S(1)}, f32[9,74,128]{2,1,0:T(8,128)S(1)}, u32[]{:S(2)}, u32[]{:S(2)}) collective-permute-start(f32[9,74,128]{2,1,0:T(8,128)S(1)} %get-tuple-element.6), channel_id=1, source_target_pairs={{14,0},{0,2},{2,4},{4,6},{6,8},{8,10},{10,12},{12,14},{15,1},{1,3}... | collective-permute-start | bytes 1022984 | tf_op jit(solution)/shard_map/ppermute | solution.py:149
  67.8 29.5 %collective-permute-start.3 = (f32[9,74,128]{2,1,0:T(8,128)S(1)}, f32[9,74,128]{2,1,0:T(8,128)S(1)}, u32[]{:S(2)}, u32[]{:S(2)}) collective-permute-start(f32[9,74,128]{2,1,0:T(8,128)S(1)} %get-tuple-element.7), channel_id=1, source_target_pairs={{2,0},{4,2},{6,4},{8,6},{10,8},{12,10},{14,12},{0,14},{3,1},{5,3},... | collective-permute-start | bytes 1022984 | tf_op jit(solution)/shard_map/ppermute | solution.py:149
